TPU v7x, 256 devices: a whole 4x4x8 slice. The times are simulated.
256 devices in a mesh: scen: 4 (over x_lo, core), row: 8 (over x_hi, y), col: 8 (over z).
Axes of the slice: x: 4 (x_hi: 2, x_lo: 2; x = x_hi * 2 + x_lo), y: 4, z: 8, core: 2. Of those that a mesh axis runs over, the one named last changes fastest.
Arguments:
- link_block: float32 [2560, 2, 8, 8, 128], P('scen', None, 'row', 'col'), may hold values from -0.15625 to 0.15625
- block_mask: int32 [32, 2, 8, 8], P('scen', None, 'row', 'col'), may hold values 0 or 1
- barrier_diag: float32 [2560], P('scen'), may hold values from 0.1 to 10
- first_section_diag: float32 [2, 8, 8, 128], P(None, 'row', 'col'), may hold values from 0.5 to 1.5
Outputs:
- factored: float32 [2, 8, 8, 128, 2, 8, 8, 128], P(None, 'row', 'scen', None, None, None, 'col')
All inputs are finite; a program needn't handle non-finite values. No bound on the sum of `block_mask` on one device may be relied on, other than what follows from the above.
Results may differ from a plain program's by a relative error of at most 0.0003.
Values sent between devices are 32-bit elements; how exact they have to be, the bound alone decides.
A program may use at most 128 MiB of HBM per device.

v0:
```python
import jax
import jax.numpy as jnp
from jax import lax
from jax.sharding import PartitionSpec as P

PANEL = 256


HIGH = lax.Precision.HIGHEST


def spread(block, axis, source):
    block = jnp.where(lax.axis_index(axis) == source, block, jnp.zeros_like(block))
    return lax.psum(block, axis)


def solve_right(lower, rhs):
    return jax.scipy.linalg.solve_triangular(lower, rhs.T, lower=True).T


def contract_rows(left, right):
    return lax.dot_general(
        left, right, (((0,), (0,)), ((), ())), precision=HIGH, preferred_element_type=jnp.float32
    )


def per_device(link_block, block_mask, barrier_diag, first_section_diag):
    rows_dev = link_block.shape[0]
    blocks = link_block.shape[1]
    tile = link_block.shape[4]
    scenarios = block_mask.shape[0]
    count_scen = lax.axis_size("scen")
    count_rows = lax.axis_size("row")
    count_cols = lax.axis_size("col")
    share = count_cols // count_scen
    width = 2 * PANEL
    scen_index = lax.axis_index("scen")
    row_index = lax.axis_index("row")
    col_index = lax.axis_index("col")
    per_scenario = rows_dev // scenarios
    weights = block_mask.astype(jnp.float32).reshape(scenarios, 1, blocks, 1, 1, 1)
    masked = (link_block.reshape(scenarios, per_scenario, blocks, 1, 1, tile) * weights).reshape(
        rows_dev, blocks, 1, 1, tile
    )
    scaled = masked * barrier_diag[:, None, None, None, None]
    row_side = lax.all_gather(masked, "col", axis=3, tiled=True)
    row_side = jnp.transpose(row_side, (0, 3, 1, 2, 4)).reshape(
        rows_dev, count_cols * blocks * tile
    )
    col_count = blocks * count_rows * tile
    col_side = lax.all_gather(scaled, "row", axis=2, tiled=True).reshape(rows_dev, col_count)
    local_rows = share * blocks * tile
    owned = lax.psum_scatter(
        contract_rows(row_side, col_side), "scen", scatter_dimension=0, tiled=True
    )
    schur = (
        owned.reshape(share, blocks, tile, col_count)
        .transpose(1, 0, 2, 3)
        .reshape(local_rows, col_count)
    )
    row_block = jnp.arange(blocks)[:, None, None]
    row_group = (scen_index * share + jnp.arange(share))[None, :, None]
    row_cell = jnp.arange(tile)[None, None, :]
    row_global = (
        ((row_block * count_rows + row_index) * count_cols + row_group) * tile + row_cell
    ).reshape(-1)
    col_block = jnp.arange(blocks)[:, None, None]
    col_group = jnp.arange(count_rows)[None, :, None]
    col_cell = jnp.arange(tile)[None, None, :]
    col_global = (
        ((col_block * count_rows + col_group) * count_cols + col_index) * tile + col_cell
    ).reshape(-1)
    col_diag = jnp.broadcast_to(
        first_section_diag.reshape(blocks, 1, tile), (blocks, count_rows, tile)
    ).reshape(-1)
    schur = schur + jnp.where(row_global[:, None] == col_global[None, :], col_diag[None, :], 0.0)
    lead_cols = lax.all_gather(schur[:, :tile], "col", axis=1, tiled=True)[:, :width]
    top_rows = lax.all_gather(lead_cols[: share * tile], "scen", axis=0, tiled=True)
    top = spread(top_rows, "row", 0)[:width]
    top_ids = jnp.arange(width)[:, None]
    panel_ids = jnp.arange(PANEL)[None, :]
    mine_ids = row_global[:, None]
    first_factor = jnp.linalg.cholesky(top[:PANEL, :PANEL])
    top_first = jnp.where(top_ids >= panel_ids, solve_right(first_factor, top[:, :PANEL]), 0.0)
    mine_first = jnp.where(
        mine_ids >= panel_ids, solve_right(first_factor, lead_cols[:, :PANEL]), 0.0
    )
    coupling = top_first[PANEL:]
    top_second = top[:, PANEL:] - jnp.dot(
        top_first, coupling.T, precision=HIGH, preferred_element_type=jnp.float32
    )
    second_factor = jnp.linalg.cholesky(top_second[PANEL:])
    mine_second_in = lead_cols[:, PANEL:] - jnp.dot(
        mine_first, coupling.T, precision=HIGH, preferred_element_type=jnp.float32
    )
    mine_second = jnp.where(
        mine_ids >= panel_ids + PANEL, solve_right(second_factor, mine_second_in), 0.0
    )
    mine = jnp.concatenate([mine_first, mine_second], axis=1)
    picked = lax.dynamic_index_in_dim(
        mine.reshape(blocks, share, tile, width), col_index % share, 1, keepdims=True
    )
    owner_rows = spread(picked, "scen", col_index // share)
    col_factor = lax.all_gather(owner_rows, "row", axis=1, tiled=True).reshape(col_count, width)
    update = schur - lax.dot_general(
        mine,
        col_factor,
        (((1,), (1,)), ((), ())),
        precision=HIGH,
        preferred_element_type=jnp.float32,
    )
    trailing = jnp.where(mine_ids >= width, update, schur)
    padded = jnp.pad(mine, ((0, 0), (0, count_cols * tile - width)))
    own_lead = lax.dynamic_slice_in_dim(padded, col_index * tile, tile, 1)
    first_cols = jnp.where(col_global[None, :tile] < width, own_lead, trailing[:, :tile])
    result = jnp.concatenate([first_cols, trailing[:, tile:]], axis=1)
    return result.reshape(blocks, 1, share, tile, blocks, count_rows, 1, tile)


def solution(mesh):
    placed = (
        P("scen", None, "row", "col", None),
        P("scen", None, "row", "col"),
        P("scen"),
        P(None, "row", "col", None),
    )
    return jax.shard_map(
        per_device,
        mesh=mesh,
        in_specs=placed,
        out_specs=P(None, "row", "scen", None, None, None, "col", None),
        check_vma=False,
    )
```

profile of v0, /device:TPU:5, one launch (start us, length us, event | category | flops | bytes accessed | tf_op | source)
XLA Modules:
  0.0 858.3 jit_solution(5944905493652222210)
XLA Ops:
  7.4 2.5 multiply_bitcast_fusion
  10.7 66.9 %all-gather.6.cloned.1.call-done = f32[640,2,1,8,128]{4,0,2,1,3:T(8,128)} async-done(((f32[640,2,1,1,128]{4,0,2,1,3:T(8,128)}), f32[640,2,1,8,128]{4,0,2,1,3:T(8,128)}) %all-gather.6.cloned.1.call-update) | async-done | bytes 5242896 | tf_op jit(solution)/shard_map/all_gather | solution.py:46
  77.6 5.9 copy.43
  83.5 77.7 %all-gather.8.cloned.1.call-done = f32[640,2,8,1,128]{4,0,3,1,2:T(8,128)} async-done(((f32[640,2,1,1,128]{4,0,3,1,2:T(8,128)}), f32[640,2,8,1,128]{4,0,3,1,2:T(8,128)}) %all-gather.8.cloned.1.call-update) | async-done | bytes 5242896 | tf_op jit(solution)/shard_map/all_gather | solution.py:51
  161.2 6.0 copy.45
  167.2 44.8 %fusion.31 = f32[2048,2048]{1,0:T(8,128)} fusion(f32[640,2048]{0,1:T(8,128)} %bitcast.121, f32[640,2048]{0,1:T(8,128)} %bitcast.122), kind=kOutput, calls=%fused_computation.96 | convolution fusion | flops 32212254720 | bytes 27262976 | tf_op jit(solution)/shard_map/dot_general | solution.py:22
  212.6 149.2 %reduce-scatter.2.cloned.1.call-done = f32[512,2048]{1,0:T(8,128)} async-done(((f32[2048,2048]{1,0:T(8,128)}), f32[512,2048]{1,0:T(8,128)}) %reduce-scatter.2.cloned.1.call-update) | async-done | bytes 4194320 | tf_op jit(solution)/shard_map/reduce_scatter | solution.py:53
  361.8 7.2 copy.46
  369.0 6.4 reshape.186
  375.4 2.6 select_add_fusion
  378.0 2.0 copy-done.2
  380.8 38.6 %all-gather.10.cloned.1.call-done = f32[512,1024]{0,1:T(8,128)} async-done(((f32[512,128]{0,1:T(8,128)}), f32[512,1024]{0,1:T(8,128)}) %all-gather.10.cloned.1.call-update) | async-done | bytes 2097168 | tf_op jit(solution)/shard_map/all_gather | solution.py:77
  419.4 1.9 slice.106
  421.4 34.1 %all-gather.12.cloned.1.call-done = f32[1024,512]{0,1:T(8,128)} async-done(((f32[256,512]{0,1:T(8,128)}), f32[1024,512]{0,1:T(8,128)}) %all-gather.12.cloned.1.call-update) | async-done | bytes 2097168 | tf_op jit(solution)/shard_map/all_gather | solution.py:78
  458.3 91.5 %all-reduce.5.cloned.1.call-done = f32[1024,512]{0,1:T(8,128)} async-done(((f32[1024,512]{0,1:T(8,128)}), f32[1024,512]{0,1:T(8,128)}) %all-reduce.5.cloned.1.call-update) | async-done | bytes 2097168 | tf_op jit(solution)/shard_map/psum | solution.py:14
  551.9 11.7 %cholesky.130 = f32[128,128]{1,0:T(8,128)S(1)} custom-call(f32[128,128]{1,0:T(8,128)S(1)} %cholesky.194), custom_call_target="Cholesky" | custom-call | tf_op jit(solution)/shard_map/jit(cholesky)/cholesky | solution.py:83
  563.7 9.8 %custom-call.14 = f32[1,128,128]{1,2,0:T(8,128)S(1)} custom-call(f32[1,128,128]{2,1,0:T(8,128)S(1)} %get-tuple-element.61), custom_call_target="InvertDiagBlocksLowerTriangular" | custom-call | tf_op jit(solution)/shard_map/jit(cholesky)/cholesky | solution.py:83
  574.0 11.7 %cholesky.147 = f32[128,128]{1,0:T(8,128)S(1)} custom-call(f32[128,128]{1,0:T(8,128)S(1)} %convolution_subtract_fusion.5), custom_call_target="Cholesky" | custom-call | tf_op jit(solution)/shard_map/jit(cholesky)/cholesky | solution.py:83
  588.3 14.0 %while.6 = (s32[]{:T(128)}, f32[256,256]{1,0:T(8,128)S(1)}, s32[2,2]{1,0:T(2,128)S(1)}, f32[2,128,128]{2,1,0:T(8,128)S(1)}, s32[]{:T(128)}) while((s32[]{:T(128)}, f32[256,256]{1,0:T(8,128)S(1)}, s32[2,2]{1,0:T(2,128)S(1)}, f32[2,128,128]{2,1,0:T(8,128)S(1)}, s32[]{:T(128)}) %tuple.48), condition=%wide.while_cond, body=%wide.while_body.sunk | while | flops 2 | bytes 131189 | solution.py:18
  602.3 19.7 %custom-call.15 = f32[2,128,128]{1,2,0:T(8,128)S(1)} custom-call(f32[2,128,128]{2,1,0:T(8,128)S(1)} %get-tuple-element.27), custom_call_target="InvertDiagBlocksLowerTriangular" | custom-call | tf_op jit(solution)/shard_map/jit(_solve_triangular)/triangular_solve | solution.py:18
  626.7 11.7 %cholesky.164 = f32[128,128]{1,0:T(8,128)S(1)} custom-call(f32[128,128]{1,0:T(8,128)S(1)} %cholesky.197), custom_call_target="Cholesky" | custom-call | tf_op jit(solution)/shard_map/jit(cholesky)/cholesky | solution.py:92
  638.5 9.8 %custom-call.17 = f32[1,128,128]{1,2,0:T(8,128)S(1)} custom-call(f32[1,128,128]{2,1,0:T(8,128)S(1)} %get-tuple-element.57), custom_call_target="InvertDiagBlocksLowerTriangular" | custom-call | tf_op jit(solution)/shard_map/jit(cholesky)/cholesky | solution.py:92
  648.8 11.9 %cholesky.181 = f32[128,128]{1,0:T(8,128)S(1)} custom-call(f32[128,128]{1,0:T(8,128)S(1)} %convolution_subtract_fusion.4), custom_call_target="Cholesky" | custom-call | tf_op jit(solution)/shard_map/jit(cholesky)/cholesky | solution.py:92
  663.5 4.1 while.7
  667.5 19.7 %custom-call.18 = f32[2,128,128]{1,2,0:T(8,128)S(1)} custom-call(f32[2,128,128]{2,1,0:T(8,128)S(1)} %get-tuple-element.29), custom_call_target="InvertDiagBlocksLowerTriangular" | custom-call | tf_op jit(solution)/shard_map/jit(_solve_triangular)/triangular_solve | solution.py:18
  694.4 48.7 %all-reduce.7.cloned.1.call-done = f32[2,1,128,512]{3,2,0,1:T(8,128)} async-done(((f32[2,1,128,512]{3,2,0,1:T(8,128)}), f32[2,1,128,512]{3,2,0,1:T(8,128)}) %all-reduce.7.cloned.1.call-update) | async-done | bytes 524304 | tf_op jit(solution)/shard_map/psum | solution.py:14
  743.2 77.4 %all-gather.14.cloned.1.call-done = f32[2,8,128,512]{3,2,0,1:T(8,128)} async-done(((f32[2,1,128,512]{3,2,0,1:T(8,128)}), f32[2,8,128,512]{3,2,0,1:T(8,128)}) %all-gather.14.cloned.1.call-update) | async-done | bytes 4194320 | tf_op jit(solution)/shard_map/all_gather | solution.py:104
  820.6 3.0 copy.52
  824.0 7.3 subtract_select_fusion
  831.8 2.5 pad_maximum_fusion
  834.3 5.9 reshape.189
  840.2 10.9 %copy.54 = f32[2,1,2,128,2,8,1,128]{7,6,5,4,3,2,1,0:T(1,128)} copy(f32[2,1,2,128,2,8,1,128]{3,2,0,7,5,4,6,1:T(2,128)} %reshape.189) | data formatting | bytes 8388608 | tf_op jit(solution)/shard_map/reshape | solution.py:117
  (101 shorter events, 32.4 us)
Async XLA Ops:
  6.5 206.0 %copy-start = (f32[2,1,1,128]{3,2,1,0:T(1,128)S(1)}, f32[2,1,1,128]{3,2,1,0:T(1,128)}, u32[]{:S(2)}) copy-start(f32[2,1,1,128]{3,2,1,0:T(1,128)} %param.10) | copy-start | bytes 3076
  6.5 71.1 %all-gather.6.cloned.1.call-start = ((), (), s32[]{:S(2)}) async-start(), calls=%async_computation.1 | async-start | bytes 5898240 | tf_op jit(solution)/shard_map/all_gather | solution.py:46
  9.9 151.3 %all-gather.8.cloned.1.call-start = ((), (), s32[]{:S(2)}) async-start(), calls=%async_computation.2 | async-start | bytes 5898240 | tf_op jit(solution)/shard_map/all_gather | solution.py:51
  10.6 351.2 %reduce-scatter.2.cloned.1.call-start = ((), (), s32[]{:S(2)}) async-start(), calls=%async_computation.3 | async-start | bytes 20971520 | tf_op jit(solution)/shard_map/reduce_scatter | solution.py:53
  212.0 207.4 %all-gather.10.cloned.1.call-start = ((), (), s32[]{:S(2)}) async-start(), calls=%async_computation.4 | async-start | bytes 2359296 | tf_op jit(solution)/shard_map/all_gather | solution.py:77
  378.0 2.0 copy-start.2
  380.8 74.7 %all-gather.12.cloned.1.call-start = ((), (), s32[]{:S(2)}) async-start(), calls=%async_computation.5 | async-start | bytes 2621440 | tf_op jit(solution)/shard_map/all_gather | solution.py:78
  421.3 128.5 %all-reduce.5.cloned.1.call-start = ((), (), s32[]{:S(2)}) async-start(), calls=%async_computation.6 | async-start | bytes 4194304 | tf_op jit(solution)/shard_map/psum | solution.py:14
  457.1 286.0 %all-reduce.7.cloned.1.call-start = ((), (), s32[]{:S(2)}) async-start(), calls=%async_computation.7 | async-start | bytes 1048576 | tf_op jit(solution)/shard_map/psum | solution.py:14
  694.4 126.2 %all-gather.14.cloned.1.call-start = ((), (), s32[]{:S(2)}) async-start(), calls=%async_computation.8 | async-start | bytes 4718592 | tf_op jit(solution)/shard_map/all_gather | solution.py:104
  820.6 3.4 copy-start.3
  834.3 16.8 %copy-start.1 = (f32[2,1,1,128]{3,2,1,0:T(1,128)S(1)}, f32[2,1,1,128]{3,2,1,0:T(1,128)}, u32[]{:S(2)}) copy-start(f32[2,1,1,128]{3,2,1,0:T(1,128)} %param.10) | copy-start | bytes 3076
Sparse Core Ops, SparseCore 0:
  10.0 67.5 all-gather.5
  80.2 80.9 all-gather.7
  212.1 149.7 reduce-scatter.1
  380.9 38.4 all-gather.9
  421.4 34.0 all-gather.11
  458.2 91.5 all-reduce.4
  694.5 48.5 all-reduce.6
  746.1 74.3 all-gather.13
where the time goes:
time: 871 us; the launch traced here: 858 us
  waiting for transfers between devices  585 us (67%)
  other arithmetic  121 us (14%)
  local copies, waits for them, and re-layouts  65.5 us (8%)
  matrix products  59 us (7%)
  between operations  16.8 us (2%)
  loops' own time  10.3 us (1%)
    reduce_scatter x1, waiting for transfers between devices, per_device(): lax.psum_scatter(contract_rows(row_side, col_side), 'scen', scatter_dimen...  149 us
    psum x2, waiting for transfers between devices, spread(): return lax.psum(block, axis)  140 us
    all_gather x1, waiting for transfers between devices, per_device(): lax.all_gather(scaled, 'row', axis=2, tiled=True)  77.7 us
    all_gather x1, waiting for transfers between devices, per_device(): lax.all_gather(owner_rows, 'row', axis=1, tiled=True)  77.4 us
    all_gather x1, waiting for transfers between devices, per_device(): row_side = lax.all_gather(masked, 'col', axis=3, tiled=True)  66.9 us
    dot_general x1, matrix products, contract_rows(): lax.dot_general(left, right, (((0,), (0,)), ((), ())), precision=HIGH, pr...  44.8 us
    another operation x5, other arithmetic, solve_right(): return jax.scipy.linalg.solve_triangular(lower, rhs.T, lower=True).T  39.4 us
    all_gather x1, waiting for transfers between devices, per_device(): lax.all_gather(schur[:, :tile], 'col', axis=1, tiled=True)[:, :width]  38.6 us
  transfers between devices with their start and end apart: 8, of which 8 were waited for; matrix products, arithmetic and copies ran while one was open for 1% of the time, Pallas kernels for 0%

commit v1 on v0

v1 whole, which is shorter than its diff:
```python
import functools
import jax
import jax.numpy as jnp
from jax import lax
from jax.experimental import pallas as pl
from jax.experimental.pallas import tpu as pltpu
from jax.sharding import PartitionSpec as P

PANEL = 256
F32 = jnp.float32
BF16 = jnp.bfloat16
KL = 640
KP = 648
HALVES = ((0, 320), (320, 328))


def place():
    s = lax.axis_index("scen")
    r = lax.axis_index("row")
    z = lax.axis_index("col")
    return (r // 4) * 2 + s // 2, r % 4, z, s % 2


def device(x, y, z, p):
    return ((x % 2) * 2 + p, (x // 2) * 4 + y, z)


def remote(src, dst, send, recv, to):
    return pltpu.make_async_remote_copy(
        src_ref=src, dst_ref=dst, send_sem=send, recv_sem=recv,
        device_id=to, device_id_type=pl.DeviceIdType.MESH,
    )


def split(v):
    hi = v.astype(BF16)
    return hi, (v - hi.astype(F32)).astype(BF16)


def mm(a, b):
    return jnp.dot(a, b, preferred_element_type=F32)


def nt(a, b):
    return lax.dot_general(a, b, (((1,), (1,)), ((), ())), preferred_element_type=F32)


def dot32(a, b):
    return jnp.dot(a, b, precision=lax.Precision.HIGHEST, preferred_element_type=F32)


def factor_tile(t):
    lanes = lax.broadcasted_iota(jnp.int32, (8, 128), 1)
    for p in range(0, 128, 8):
        n = 128 - p
        cols = [jnp.broadcast_to(t[p:128, p + j:p + j + 1], (n, 128)) for j in range(8)]
        row = t[p:p + 8, :]
        subl = lax.broadcasted_iota(jnp.int32, (8, 128), 0)
        us, rs_ = [], []
        for j in range(8):
            inv = lax.rsqrt(cols[j][j:j + 1, :])
            u = cols[j] * inv
            r = jnp.where(lanes[0:1] == p + j, inv, row[j:j + 1, :] * inv)
            scal = [u[m:m + 1, :] for m in range(8)]
            for m in range(j + 1, 8):
                cols[m] = cols[m] - u * scal[m]
            uj = jnp.where(subl > j, u[0:8, :], 0.0)
            base = jnp.where(jnp.logical_and(lanes == p + j, subl > j), 0.0, row)
            row = jnp.where(subl == j, jnp.broadcast_to(r, (8, 128)), base - uj * r)
            us.append(u)
        t[p:p + 8, :] = row
        if n > 8:
            rest = t[p + 8:128, :]
            rl_ = lax.broadcasted_iota(jnp.int32, (n - 8, 128), 1)
            rest = jnp.where(jnp.logical_and(rl_ >= p, rl_ < p + 8), 0.0, rest)
            for j in range(8):
                r = jnp.where(jnp.logical_and(lanes[0:1] > p + j, lanes[0:1] < p + 8), 0.0, row[j:j + 1, :])
                rest = rest - us[j][8:, :] * r
            t[p + 8:128, :] = rest


def factor_lead(m, t):
    ii = lax.broadcasted_iota(jnp.int32, (128, 128), 0)
    jj = lax.broadcasted_iota(jnp.int32, (128, 128), 1)
    for k in range(4):
        a, e = k * 128, (k + 1) * 128
        t[...] = m[a:e, a:e]
        factor_tile(t)
        inv = jnp.where(ii >= jj, t[...], 0.0)
        m[a:e, a:e] = inv
        for j in range(4):
            if j != k:
                m[a:e, j * 128:(j + 1) * 128] = dot32(inv, m[a:e, j * 128:(j + 1) * 128])
        for i in range(k + 1, 4):
            ut = m[a:e, i * 128:(i + 1) * 128].T
            for j in range(4):
                c = slice(j * 128, (j + 1) * 128)
                v = dot32(ut, m[a:e, c])
                r = slice(i * 128, (i + 1) * 128)
                if j == k:
                    m[r, c] = -v
                elif j < k or j >= i or True:
                    m[r, c] = m[r, c] - v


def schur_kernel(
    b, out, rbuf, lbuf, lthi, ltlo, rh, rl, pbuf, qbuf, s_out,
    gsend, grecv, tile, wbuf, li, ms, mf, lih, lil, mfh, mfl,
    s1, sp, s2, s3, sz, sf, sx, rsem, rsem2, lsem, xsem,
    gsem, wsend, wrecv, lsend, lrecv, wsib, lsib, msend, mrecv,
):
    x, y, z, p = place()
    xn = lambda d: device((x + d) % 4, y, z, p)
    yn = lambda d: device(x, (y + d) % 4, z, p)
    zup = device(x, y, (z + 1) % 8, p)
    zdn = device(x, y, (z + 7) % 8, p)
    peer_x = x + 1 - 2 * (x % 2)
    peer = device(peer_x, y, z, p)
    sib = device(x, y, z, 1 - p)
    x_lo = x % 2
    rel = (z + 8 - 4 * x_lo) % 8
    is_src = rel < 4

    is_root = jnp.logical_and(x == 0, y == 0)
    others = jnp.logical_not(is_root)

    barrier = pltpu.get_barrier_semaphore()
    partners = [device((x + i) % 4, (y + j) % 4, z, p) for i in range(4) for j in range(4) if i or j]
    partners += [zup, zdn, sib]
    for to in partners:
        pl.semaphore_signal(barrier, inc=1, device_id=to, device_id_type=pl.DeviceIdType.MESH)
    pl.semaphore_wait(barrier, len(partners))

    full = pl.ds(0, KL)
    sends = []

    def go(copy, cond=None):
        if cond is None:
            copy.start()
        else:
            pl.when(cond)(copy.start)
        sends.append((copy, cond))

    def wait_on(ref, sem):
        pltpu.make_async_copy(ref, ref, sem).wait()

    for a in range(2):
        for h, (lo, n) in enumerate(HALVES):
            rows = pl.ds(lo, n)
            go(remote(b.at[a, rows], lbuf.at[a, x_lo, z % 4, rows], sp.at[a, h],
                      lsem.at[a, x_lo, z % 4, h], peer), jnp.logical_not(is_src))
    for d in (1, 3, 2):
        go(remote(b.at[0, full], rbuf.at[0, x, y], s1.at[0, d - 1], rsem.at[0, x, y], xn(d)))
        go(remote(b.at[1, full], rbuf.at[1, x, y], s1.at[1, d - 1], rsem.at[1, x, y], yn(d)))

    def own(a):
        rbuf[a, x, y] = b[a, 0:KL, :]

    own(0)
    own(1)

    @pl.when(is_src)
    def _():
        for a in range(2):
            lbuf[a, x_lo, z % 4] = b[a]

    up_of = lambda i: jnp.where(i < 2, 2, 5)

    def zsend(q, xl, cond):
        a = q
        for h, (lo, n) in enumerate(HALVES):
            rows = pl.ds(lo, n)
            for dr, to in ((0, zup), (1, zdn)):
                ref = lbuf.at[a, xl, z % 4, rows]
                k = jnp.where(xl == x_lo, 0, 1)
                go(remote(ref, ref, sz.at[a, k, h, dr], lsem.at[a, xl, z % 4, h], to), cond)

    def stage2_send(a, k, d):
        ref = rbuf.at[0, (x + d) % 4, y] if a == 0 else rbuf.at[1, x, (y + d) % 4]
        sem = rsem.at[0, (x + d) % 4, y] if a == 0 else rsem.at[1, x, (y + d) % 4]
        if d:
            wait_on(ref, sem)
        step = yn if a == 0 else xn
        go(remote(ref, ref, s2.at[a, k, 0], sem, step(1)))
        go(remote(ref, ref, s2.at[a, k, 1], sem, step(3)))

    def stage2_forward(a, k, d):
        for dr, e in ((0, 3), (1, 1)):
            i = ((x + d) % 4, (y + e) % 4) if a == 0 else ((x + e) % 4, (y + d) % 4)
            ref = rbuf.at[a, i[0], i[1]]
            wait_on(ref, rsem.at[a, i[0], i[1]])
            rows = pl.ds(dr * 320, 320)
            ref = rbuf.at[a, i[0], i[1], rows]
            sem = (rsem2.at[a, i[0], i[1], dr])
            step = yn if a == 0 else xn
            go(remote(ref, ref, s3.at[a, k, dr], sem, step(1 if dr == 0 else 3)))

    def stage2_last(a, d):
        for dr in range(2):
            i = ((x + d) % 4, (y + 2) % 4) if a == 0 else ((x + 2) % 4, (y + d) % 4)
            wait_on(rbuf.at[a, i[0], i[1], pl.ds(dr * 320, 320)], rsem2.at[a, i[0], i[1], dr])

    def zforward(d):
        for a in range(2):
            for xl in range(2):
                for h, (lo, n) in enumerate(HALVES):
                    rows = pl.ds(lo, n)
                    for dr, to in ((0, zup), (1, zdn)):
                        i = (rel + 8 - d) % 8 if dr == 0 else (rel + d) % 8
                        reach = up_of(i) if dr == 0 else 7 - up_of(i)
                        slot = i % 4
                        valid = jnp.logical_and(i < 4, d <= reach)
                        ref = lbuf.at[a, xl, slot, rows]
                        sem = lsem.at[a, xl, slot, h]

                        @pl.when(valid)
                        def _():
                            wait_on(ref, sem)

                        if d < 5:
                            go(remote(ref, ref, sf.at[d - 1, a, xl, h, dr], sem, to),
                               jnp.logical_and(i < 4, d < reach))

    for a in range(2):
        zsend(a, x_lo, is_src)
    for a in range(2):
        stage2_send(a, 0, 0)
    for a in range(2):
        for h, (lo, n) in enumerate(HALVES):
            @pl.when(is_src)
            def _():
                wait_on(lbuf.at[a, 1 - x_lo, z % 4, pl.ds(lo, n)], lsem.at[a, 1 - x_lo, z % 4, h])
        zsend(a, 1 - x_lo, is_src)
    for k, d in ((1, 1), (2, 3)):
        for a in range(2):
            stage2_send(a, k, d)
    zforward(1)
    for a in range(2):
        stage2_send(a, 3, 2)
        stage2_forward(a, 0, 0)
    zforward(2)
    for k, d in ((1, 1), (2, 3)):
        for a in range(2):
            stage2_forward(a, k, d)
    zforward(3)
    for a in range(2):
        stage2_forward(a, 3, 2)
    zforward(4)
    zforward(5)
    for d in range(4):
        for a in range(2):
            stage2_last(a, d)

    @pl.loop(0, 4)
    def _(hh):
        for a in range(2):
            for xl in range(2):
                hi, lo = split(lbuf[a, xl, hh, 0:KL, :].T)
                rb = pl.multiple_of(((hh // 2) * 4 + a * 2 + hh % 2) * 128, 128)
                lthi[pl.ds(rb, 128), xl * KL:(xl + 1) * KL] = hi
                ltlo[pl.ds(rb, 128), xl * KL:(xl + 1) * KL] = lo

    gcopy = remote(gsend, grecv, gsem.at[0], gsem.at[1], sib)

    @pl.when(is_root)
    def _():
        for j in range(2):
            lead = slice(j * 512, j * 512 + 256)
            cols = slice(j * 256, j * 256 + 256)

            def gram(rows):
                return nt(lthi[rows, :], lthi[lead, :]) + nt(lthi[rows, :], ltlo[lead, :]) + nt(ltlo[rows, :], lthi[lead, :])

            for i in range(2):
                gsend[i * 256:i * 256 + 256, cols] = gram(slice(i * 512, i * 512 + 256))
            there = pl.multiple_of((1 - p) * 512 + 256, 256)
            here = pl.multiple_of(p * 512 + 256, 256)
            gsend[512:768, cols] = gram(pl.ds(there, 256))
            for c in range(2):
                ms[j * 2 + c, 256:512, :] = gram(pl.ds(here, 256))[:, c * 128:(c + 1) * 128]
        gcopy.start()

    def sib_copy(a, g):
        rows = pl.ds(a * 256, 256)
        return remote(pbuf.at[g, rows], qbuf.at[g, rows], sx.at[a, g], xsem.at[a, g], sib)

    def product(a):
        @pl.loop(0, 8)
        def _(g):
            for xl in range(2):
                for c in range(2):
                    hi, lo = split(rbuf[c, (g // 4) * 2 + xl, g % 4])
                    rh[xl * KL:(xl + 1) * KL, c * 128:(c + 1) * 128] = hi
                    rl[xl * KL:(xl + 1) * KL, c * 128:(c + 1) * 128] = lo
            for t in range(2):
                q = (1 - p) if t == 0 else p
                rows = pl.ds(pl.multiple_of(q * 512 + a * 256, 256), 256)
                v = mm(lthi[rows, :], rh[...]) + mm(ltlo[rows, :], rh[...]) + mm(lthi[rows, :], rl[...])
                if t == 0:
                    pbuf[g, a * 256:(a + 1) * 256, :] = v
                    sib_copy(a, g).start()
                else:
                    s_out[g, a * 256:(a + 1) * 256, :] = v

    def combine(a):
        rows = slice(a * 256, a * 256 + 256)

        @pl.loop(0, 8)
        def _(g):
            sib_copy(a, g).wait_recv()
            s_out[g, rows, :] = s_out[g, rows, :] + qbuf[g, rows, :]

        @pl.when(z // 2 == x_lo * 2 + p)
        def _():
            ii = lax.broadcasted_iota(jnp.int32, (128, 128), 0)
            jj = lax.broadcasted_iota(jnp.int32, (128, 128), 1)
            g = (x // 2) * 4 + y
            here = pl.ds(pl.multiple_of(a * 256 + (z % 2) * 128, 128), 128)
            diag = jnp.where(ii == jj, b[a, KL:KL + 1, :], 0.0)
            s_out[g, here, a * 128:(a + 1) * 128] += diag

    def not_root(i, j):
        return jnp.logical_not(jnp.logical_and(i == 0, j == 0))

    def make_spread(piece, send, recv):
        def copy(i, j, to_i, to_j, slot):
            ref = piece(i, j)
            return remote(ref, ref, send.at[slot], recv.at[i, j], device(to_i, to_j, z, p))

        def scatter():
            for k in range(1, 16):
                go(copy(k // 4, k % 4, k // 4, k % 4, k), is_root)

        def arrived(i, j):
            pl.when(others)(lambda: wait_on(piece(i, j), recv.at[i, j]))

        def along_x():
            arrived(x, y)
            for d in (1, 3, 2):
                i = (x + d) % 4
                go(copy(x, y, i, y, 15 + d), not_root(i, y))

        def along_y():
            for e in range(4):
                i = (x + e) % 4
                if e:
                    arrived(i, y)
                for d in (1, 3, 2):
                    j = (y + d) % 4
                    go(copy(i, y, x, j, 18 + 3 * e + d), not_root(x, j))

        def finish():
            for d in (1, 3, 2):
                for e in range(4):
                    arrived((x + e) % 4, (y + d) % 4)

        return scatter, along_x, along_y, finish

    w_scatter, w_along_x, w_along_y, w_finish = make_spread(
        lambda i, j: wbuf.at[p, (i * 4 + j) // 2, j % 2], wsend, wrecv)
    l_scatter, l_along_x, l_along_y, l_finish = make_spread(
        lambda i, j: li.at[pl.ds(pl.multiple_of(p * 256 + (i * 4 + j) * 16, 16), 16)], lsend, lrecv)

    product(0)
    combine(0)

    @pl.when(is_root)
    def _():
        for g in range(8):
            for hl in range(2):
                wbuf[p, g, hl] = s_out[g, hl * 128:(hl + 1) * 128, :]

    w_scatter()
    product(1)
    combine(1)

    ms_ref = lambda c: ms.at[c]

    @pl.when(jnp.logical_and(others, z < 4))
    def _():
        ms[z % 4] = s_out[0, :, 0:128]

    src = jnp.logical_and(others, z < 4)
    for dr, to in ((0, zup), (1, zdn)):
        ref = ms.at[z % 4]
        go(remote(ref, ref, msend.at[0, dr], mrecv.at[z % 4], to), src)
    w_along_x()
    w_along_y()
    for d in range(1, 6):
        for dr, to in ((0, zup), (1, zdn)):
            i = (z + 8 - d) % 8 if dr == 0 else (z + d) % 8
            reach = up_of(i) if dr == 0 else 7 - up_of(i)
            ref = ms.at[i % 4]
            sem = mrecv.at[i % 4]
            pl.when(jnp.logical_and(others, jnp.logical_and(i < 4, d <= reach)))(
                functools.partial(wait_on, ref, sem))
            if d < 5:
                go(remote(ref, ref, msend.at[d, dr], sem, to),
                   jnp.logical_and(others, jnp.logical_and(i < 4, d < reach)))

    ii = lax.broadcasted_iota(jnp.int32, (128, 128), 0)
    jj = lax.broadcasted_iota(jnp.int32, (128, 128), 1)

    @pl.when(is_root)
    def _():
        gcopy.wait()
        li[...] = gsend[0:512, :] + grecv[0:512, :]
        for h in range(4):
            c = slice(h * 128, (h + 1) * 128)
            li[c, c] += jnp.where(ii == jj, lbuf[0, 0, h, KL:KL + 1, :], 0.0)
        for c in range(4):
            lanes = slice(c * 128, (c + 1) * 128)
            ms[c, 0:256, :] = li[pl.ds(pl.multiple_of(p * 256, 256), 256), lanes]
            ms[c, 256:512, :] += grecv[512:768, lanes]
        factor_lead(li, tile)
        for i in range(3):
            li[i * 128:(i + 1) * 128, (i + 1) * 128:512] = jnp.zeros((128, 384 - 128 * i), F32)

    l_scatter()
    l_along_x()
    w_finish()
    wcopy = remote(wbuf.at[p], wbuf.at[p], wsib.at[0], wsib.at[1], sib)
    wcopy.start()
    l_along_y()
    l_finish()
    mine_half = li.at[pl.ds(pl.multiple_of(p * 256, 256), 256)]
    lcopy = remote(mine_half, mine_half, lsib.at[0], lsib.at[1], sib)
    pl.when(others)(lcopy.start)
    wait_on(wbuf.at[1 - p], wsib.at[1])
    pl.when(others)(lambda: wait_on(li.at[pl.ds(pl.multiple_of((1 - p) * 256, 256), 256)], lsib.at[1]))

    hi, lo = split(li[...])
    lih[...] = hi
    lil[...] = lo
    row_ids = (x // 2) * 4 + y
    for k in range(4):
        n = (k + 1) * 128
        krows = slice(k * 128, n)
        acc = jnp.zeros((512, 128), F32)
        for c in range(k + 1):
            hi, lo = split(ms[c])
            cc = slice(c * 128, (c + 1) * 128)
            acc += nt(hi, lih[krows, cc]) + nt(lo, lih[krows, cc]) + nt(hi, lil[krows, cc])
        ri = lax.broadcasted_iota(jnp.int32, (512, 128), 0)
        ki = lax.broadcasted_iota(jnp.int32, (512, 128), 1) + k * 128
        rows_at = (((ri // 256) * 8 + row_ids) * 8 + (x_lo * 2 + p) * 2 + (ri // 128) % 2) * 128 + ri % 128
        acc = jnp.where(rows_at >= ki, acc, 0.0)
        hi, lo = split(acc)
        mfh[:, krows] = hi
        mfl[:, krows] = lo
        mf[k] = acc

    keep = jnp.logical_and(is_root, x_lo == 0)

    @pl.loop(0, 8)
    def _(g):
        hs, ls = [], []
        for q in range(2):
            for hl in range(2):
                hi, lo = split(wbuf[q, g, hl])
                hs.append(hi)
                ls.append(lo)
        wh = jnp.concatenate(hs, axis=0)
        wl = jnp.concatenate(ls, axis=0)
        f = mm(lih[...], wh) + mm(lil[...], wh) + mm(lih[...], wl)
        fh, fl = split(f)
        for a in range(2):
            rows = slice(a * 256, (a + 1) * 256)
            v = mm(mfh[rows, :], fh) + mm(mfl[rows, :], fh) + mm(mfh[rows, :], fl)
            sv = s_out[g, rows, :]
            v = jnp.where(jnp.logical_and(keep, a == 0), sv, sv - v)
            for c in range(2):
                out[pl.ds(a * 256 * 16 + c * 8 + g, 256, stride=16), :] = v[:, c * 128:(c + 1) * 128]

    for c in range(4):
        @pl.when(z == c)
        def _():
            out[pl.ds(0, 512, stride=16), :] = mf[c]

    for copy, cond in sends:
        if cond is None:
            copy.wait_send()
        else:
            pl.when(cond)(copy.wait_send)

    @pl.loop(0, 8)
    def _(g):
        for a in range(2):
            sib_copy(a, g).wait_send()

    wcopy.wait_send()
    pl.when(others)(lcopy.wait_send)


def schur_call(b):
    dma = pltpu.SemaphoreType.DMA
    vmem = pltpu.VMEM
    return pl.pallas_call(
        schur_kernel,
        out_shape=jax.ShapeDtypeStruct((8192, 128), F32),
        in_specs=[pl.BlockSpec(memory_space=pltpu.VMEM)],
        out_specs=pl.BlockSpec(memory_space=pltpu.VMEM),
        scratch_shapes=[
            vmem((2, 4, 4, KL, 128), F32), vmem((2, 2, 4, KP, 128), F32),
            vmem((1024, 2 * KL), BF16), vmem((1024, 2 * KL), BF16),
            vmem((2 * KL, 256), BF16), vmem((2 * KL, 256), BF16),
            vmem((8, 512, 256), F32), vmem((8, 512, 256), F32), vmem((8, 512, 256), F32),
            vmem((768, 512), F32), vmem((768, 512), F32), vmem((128, 128), F32),
            vmem((2, 8, 2, 128, 256), F32), vmem((512, 512), F32), vmem((4, 512, 128), F32), vmem((4, 512, 128), F32),
            vmem((512, 512), BF16), vmem((512, 512), BF16), vmem((512, 512), BF16), vmem((512, 512), BF16),
            dma((2, 3)), dma((2, 2)), dma((2, 4, 2)), dma((2, 4, 2)), dma((2, 2, 2, 2)),
            dma((4, 2, 2, 2, 2)), dma((2, 8)),
            dma((2, 4, 4)), dma((2, 4, 4, 2)), dma((2, 2, 4, 2)), dma((2, 8)),
            dma((2,)), dma((31,)), dma((4, 4)), dma((31,)), dma((4, 4)), dma((2,)), dma((2,)),
            dma((5, 2)), dma((4,)),
        ],
        compiler_params=pltpu.CompilerParams(
            collective_id=0, has_side_effects=True, vmem_limit_bytes=60 * 2**20
        ),
        name="schur_factor",
    )(b)


def scaled_blocks(link_block, block_mask, barrier_diag, first_section_diag):
    scen = block_mask.shape[0]
    w = block_mask.astype(F32).reshape(scen, 1, 2, 1) * jnp.sqrt(barrier_diag).reshape(scen, -1, 1, 1)
    v = (link_block.reshape(scen, -1, 2, 128) * w).reshape(KL, 2, 128).transpose(1, 0, 2)
    d = first_section_diag.reshape(2, 1, 128)
    return jnp.concatenate([v, d, jnp.zeros((2, KP - KL - 1, 128), F32)], axis=1)


def per_device(link_block, block_mask, barrier_diag, first_section_diag):
    b = scaled_blocks(link_block, block_mask, barrier_diag, first_section_diag)
    return schur_call(b).reshape(2, 1, 2, 128, 2, 8, 1, 128)


def solution(mesh):
    placed = (
        P("scen", None, "row", "col", None),
        P("scen", None, "row", "col"),
        P("scen"),
        P(None, "row", "col", None),
    )
    return jax.shard_map(
        per_device,
        mesh=mesh,
        in_specs=placed,
        out_specs=P(None, "row", "scen", None, None, None, "col", None),
        check_vma=False,
    )
```

time: 871 us -> 253 us (0.29); the launches traced: 858 us -> 253 us
  waiting for transfers between devices: 585 us -> 0 us
  Pallas kernels: 0 us -> 240 us
  other arithmetic: 121 us -> 3.68 us
  matrix products: 59 us -> 0 us
  local copies, waits for them, and re-layouts: 65.5 us -> 8.69 us
  between operations: 16.8 us -> 0.04 us
  loops' own time: 10.3 us -> 0 us
    all_gather x5 -> x0, waiting for transfers between devices: 295 us -> none  [the longest x1 77.7 us: per_device(): lax.all_gather(scaled, 'row', axis=2, tiled=True)]
    pallas_call x0 -> x1, Pallas kernels: none -> 240 us  [schur_call(): pl.pallas_call(schur_kernel, out_shape=jax.ShapeDtypeStruct((8192, 128),...]
    reduce_scatter x1 -> x0, waiting for transfers between devices: 149 us -> none  [per_device(): lax.psum_scatter(contract_rows(row_side, col_side), 'scen', scatter_dimen...]
    psum x2 -> x0, waiting for transfers between devices: 140 us -> none  [spread(): return lax.psum(block, axis)]
    another operation x19 -> x0, other arithmetic: 109 us -> none  [the longest x5 39.4 us: solve_right(): return jax.scipy.linalg.solve_triangular(lower, rhs.T, lower=True).T]
    dot_general x4 -> x0, matrix products: 54.5 us -> none  [the longest x1 44.8 us: contract_rows(): lax.dot_general(left, right, (((0,), (0,)), ((), ())), precision=HIGH, pr...]
    reshape x5 -> x0, local copies, waits for them, and re-layouts: 31 us -> none  [the longest x2 16.8 us: per_device(): return result.reshape(blocks, 1, share, tile, blocks, count_rows, 1, tile)]
    all_gather x3 -> x0, local copies, waits for them, and re-layouts: 14.9 us -> none  [the longest x1 5.96 us: per_device(): lax.all_gather(scaled, 'row', axis=2, tiled=True)]
  transfers between devices with their start and end apart: 8 -> 0, of which waited for: 8 -> 0; matrix products, arithmetic and copies ran while one was open for 1% -> 0% of each run, Pallas kernels for 0% -> 0%
where the time goes in v1:
time: 253 us
  Pallas kernels  240 us (95%)
  local copies, waits for them, and re-layouts  8.69 us (3%)
  other arithmetic  3.68 us (1%)
    pallas_call x1, Pallas kernels, schur_call(): pl.pallas_call(schur_kernel, out_shape=jax.ShapeDtypeStruct((8192, 128),...  240 us
    unnamed x1, local copies, waits for them, and re-layouts  7.77 us

profile of v1, /device:TPU:5, one launch (start us, length us, event | category | flops | bytes accessed | tf_op | source)
XLA Modules:
  0.0 252.6 jit_solution(81951004168523837)
XLA Ops:
  0.0 0.7 convert_element_type.3
  0.7 0.1 pad.2.clone
  0.8 0.7 sqrt.3
  1.5 0.1 mul.32
  1.5 0.1 mul.33
  1.6 1.3 fusion
  3.0 1.7 maximum_maximum_fusion.b
  4.6 240.2 %schur_factor.1 = f32[8192,128]{1,0:T(8,128)} custom-call(f32[2,648,128]{2,1,0:T(8,128)} %maximum_maximum_fusion.b), custom_call_target="tpu_custom_call" | custom-call | tf_op jit(solution)/shard_map/schur_factor/pallas_call | solution.py:498
  244.8 7.8 %copy.9 = f32[2,1,2,128,2,8,1,128]{7,6,5,4,3,2,1,0:T(1,128)} copy(f32[2,1,2,128,2,8,1,128]{7,6,5,4,3,2,1,0:T(1,128)} %bitcast.13) | data formatting | bytes 8388608
  (2 shorter events, 0.0 us)

commit v2 on v1

v2 whole, which is shorter than its diff:
```python
import functools
import jax
import jax.numpy as jnp
from jax import lax
from jax.experimental import pallas as pl
from jax.experimental.pallas import tpu as pltpu
from jax.sharding import PartitionSpec as P

PANEL = 256
F32 = jnp.float32
BF16 = jnp.bfloat16
KL = 640
KP = 648
NC = 3
CH = KP // NC
RING = 4


def place():
    s = lax.axis_index("scen")
    r = lax.axis_index("row")
    z = lax.axis_index("col")
    return (r // 4) * 2 + s // 2, r % 4, z, s % 2


def device(x, y, z, p):
    return ((x % 2) * 2 + p, (x // 2) * 4 + y, z)


def remote(src, dst, send, recv, to):
    return pltpu.make_async_remote_copy(
        src_ref=src, dst_ref=dst, send_sem=send, recv_sem=recv,
        device_id=to, device_id_type=pl.DeviceIdType.MESH,
    )


def split(v):
    hi = v.astype(BF16)
    return hi, (v - hi.astype(F32)).astype(BF16)


def mm(a, b):
    return jnp.dot(a, b, preferred_element_type=F32)


def nt(a, b):
    return lax.dot_general(a, b, (((1,), (1,)), ((), ())), preferred_element_type=F32)


def dot32(a, b):
    return jnp.dot(a, b, precision=lax.Precision.HIGHEST, preferred_element_type=F32)


def factor_tile(t):
    lanes = lax.broadcasted_iota(jnp.int32, (8, 128), 1)
    for p in range(0, 128, 8):
        n = 128 - p
        cols = [jnp.broadcast_to(t[p:128, p + j:p + j + 1], (n, 128)) for j in range(8)]
        row = t[p:p + 8, :]
        subl = lax.broadcasted_iota(jnp.int32, (8, 128), 0)
        us, rs_ = [], []
        for j in range(8):
            inv = lax.rsqrt(cols[j][j:j + 1, :])
            u = cols[j] * inv
            r = jnp.where(lanes[0:1] == p + j, inv, row[j:j + 1, :] * inv)
            scal = [u[m:m + 1, :] for m in range(8)]
            for m in range(j + 1, 8):
                cols[m] = cols[m] - u * scal[m]
            uj = jnp.where(subl > j, u[0:8, :], 0.0)
            base = jnp.where(jnp.logical_and(lanes == p + j, subl > j), 0.0, row)
            row = jnp.where(subl == j, jnp.broadcast_to(r, (8, 128)), base - uj * r)
            us.append(u)
        t[p:p + 8, :] = row
        if n > 8:
            rest = t[p + 8:128, :]
            rl_ = lax.broadcasted_iota(jnp.int32, (n - 8, 128), 1)
            rest = jnp.where(jnp.logical_and(rl_ >= p, rl_ < p + 8), 0.0, rest)
            for j in range(8):
                r = jnp.where(jnp.logical_and(lanes[0:1] > p + j, lanes[0:1] < p + 8), 0.0, row[j:j + 1, :])
                rest = rest - us[j][8:, :] * r
            t[p + 8:128, :] = rest


def factor_step(m, t, k):
    ii = lax.broadcasted_iota(jnp.int32, (128, 128), 0)
    jj = lax.broadcasted_iota(jnp.int32, (128, 128), 1)
    a, e = k * 128, (k + 1) * 128
    t[...] = m[a:e, a:e]
    factor_tile(t)
    inv = jnp.where(ii >= jj, t[...], 0.0)
    m[a:e, a:e] = inv
    for j in range(4):
        if j != k:
            m[a:e, j * 128:(j + 1) * 128] = dot32(inv, m[a:e, j * 128:(j + 1) * 128])
    for i in range(k + 1, 4):
        ut = m[a:e, i * 128:(i + 1) * 128].T
        r = slice(i * 128, (i + 1) * 128)
        for j in range(4):
            c = slice(j * 128, (j + 1) * 128)
            v = dot32(ut, m[a:e, c])
            m[r, c] = -v if j == k else m[r, c] - v


def schur_kernel(
    b, out, rbuf, lbuf, lthi, ltlo, rh, rl, pbuf, qbuf, s_out,
    gsend, grecv, tile, wbuf, li, ms, mf, lih, lil, mfh, mfl, fch, fcl,
    rs1, rs2, rs3, rr, rr2, ws1, ws2, ws3, wr, wr2, wsc, wrc,
    sp, lpeer, zs, lsem, sx, xsem, gsem, lsend, lrecv, wsib, lsib, msend, mrecv,
):
    x, y, z, p = place()
    plane = lambda i, j: device(i % 4, j % 4, z, p)
    zup = device(x, y, (z + 1) % 8, p)
    zdn = device(x, y, (z + 7) % 8, p)
    peer = device(x + 1 - 2 * (x % 2), y, z, p)
    sib = device(x, y, z, 1 - p)
    x_lo = x % 2
    rel = (z + 8 - 4 * x_lo) % 8
    is_src = rel < 4
    is_root = jnp.logical_and(x == 0, y == 0)
    others = jnp.logical_not(is_root)
    own_p = pl.multiple_of(p * 256, 256)
    sib_p = pl.multiple_of((1 - p) * 256, 256)

    barrier = pltpu.get_barrier_semaphore()
    partners = [plane(x + i, y + j) for i in range(4) for j in range(4) if i or j]
    partners += [zup, zdn, sib]
    for to in partners:
        pl.semaphore_signal(barrier, inc=1, device_id=to, device_id_type=pl.DeviceIdType.MESH)
    pl.semaphore_wait(barrier, len(partners))

    sends = []

    def go(copy, cond=None):
        if cond is None:
            copy.start()
        else:
            pl.when(cond)(copy.start)
        sends.append((copy, cond))

    def wait_on(ref, sem, cond=None):
        wait = pltpu.make_async_copy(ref, ref, sem).wait
        if cond is None:
            wait()
        else:
            pl.when(cond)(wait)

    def not_root(i, j):
        return jnp.logical_not(jnp.logical_and(i % 4 == 0, j % 4 == 0))

    class Gather:
        def __init__(self, blk, sub, s1, s2, s3, r, r2, rooted):
            self.blk, self.sub, self.s1, self.s2, self.s3, self.r, self.r2 = blk, sub, s1, s2, s3, r, r2
            self.rooted = rooted

        def at(self, a, d, e):
            return ((x + d) % 4, (y + e) % 4) if a == 0 else ((x + e) % 4, (y + d) % 4)

        def send(self, ref, send, recv, i, j):
            go(remote(ref, ref, send, recv, plane(i, j)), not_root(i, j) if self.rooted else None)

        def wait(self, ref, sem):
            wait_on(ref, sem, others if self.rooted else None)

        def first(self):
            for d in (1, 3, 2):
                for a in range(2):
                    self.send(self.blk(a, x, y), self.s1.at[a, d - 1], self.r.at[a, x, y], *self.at(a, d, 0))

        def second(self, a, k, d):
            i, j = self.at(a, d, 0)
            ref, sem = self.blk(a, i, j), self.r.at[a, i, j]
            if d:
                self.wait(ref, sem)
            self.send(ref, self.s2.at[a, k, 0], sem, *self.at(a, 0, 1))
            self.send(ref, self.s2.at[a, k, 1], sem, *self.at(a, 0, 3))

        def forward(self, a, k, d):
            for dr, e in ((0, 3), (1, 1)):
                i, j = self.at(a, d, e)
                self.wait(self.blk(a, i, j), self.r.at[a, i, j])
                line = i if a == 0 else j
                self.send(self.sub(a, i, j, dr), self.s3.at[a, k, dr], self.r2.at[a, line, dr],
                          *self.at(a, 0, 1 if dr == 0 else 3))

        def last(self, a, d):
            i, j = self.at(a, d, 2)
            line = i if a == 0 else j
            for dr in range(2):
                self.wait(self.sub(a, i, j, dr), self.r2.at[a, line, dr])

    right = Gather(
        lambda a, i, j: rbuf.at[a, i, j], lambda a, i, j, dr: rbuf.at[a, i, j, pl.ds(dr * 320, 320)],
        rs1, rs2, rs3, rr, rr2, False)
    lead = Gather(
        lambda a, i, j: wbuf.at[p, (i * 4 + j) // 2, j % 2, pl.ds(a * 64, 64)],
        lambda a, i, j, dr: wbuf.at[p, (i * 4 + j) // 2, j % 2, pl.ds(a * 64 + dr * 32, 32)],
        ws1, ws2, ws3, wr, wr2, True)

    for a in range(2):
        rbuf[a, x, y] = b[a, 0:KL, :]
        go(remote(b.at[a], lbuf.at[a, x_lo, z % 4], sp.at[a], lpeer.at[a], peer), jnp.logical_not(is_src))

    @pl.when(is_src)
    def _():
        for a in range(2):
            lbuf[a, x_lo, z % 4] = b[a]

    right.first()

    LAST = 4 * NC
    up_of = lambda i: jnp.where(i < 2, 2, 5)
    up1 = lambda v: jnp.where(jnp.logical_or(v == 0, v >= 4), 3, v - 1)
    up2 = lambda v: jnp.where(v >= 4, 2, v - 2)
    mirror = (11 - rel) % 8
    streams = []
    for dr in range(2):
        for k in range(2):
            v = rel if dr == 0 else mirror
            i = (up1 if k == 0 else up2)(v)
            valid = v >= 0 if k == 0 else v >= 2
            i = jnp.maximum(i, 0)
            d = (v + 8 - i) % 8
            src = i if dr == 0 else 3 - i
            streams.append((src, d, valid, jnp.logical_and(valid, d < up_of(i)), zup if dr == 0 else zdn))

    def zref(slot, c):
        a, k, h = c // (2 * NC), (c // NC) % 2, c % NC
        xl = (x_lo + k) % 2
        return lbuf.at[a, xl, slot, pl.ds(pl.multiple_of(h * CH, 8), CH)], lsem.at[a, xl, slot, h]

    def zsend(ref, sem, n, c, to):
        ring = zs.at[n, c % RING]

        @pl.when(c >= RING)
        def _():
            pltpu.make_async_copy(ref, ref, ring).wait()

        remote(ref, ref, ring, sem, to).start()

    def zown(c):
        @pl.when(is_src)
        def _():
            ref, sem = zref(z % 4, c)

            @pl.when(c % (2 * NC) == NC)
            def _():
                whole = lbuf.at[c // (2 * NC), 1 - x_lo, z % 4]
                pltpu.make_async_copy(whole, whole, lpeer.at[c // (2 * NC)]).wait()

            zsend(ref, sem, 4, c, zup)
            zsend(ref, sem, 5, c, zdn)

    def zstep(t):
        @pl.when(t + 2 < LAST)
        def _():
            zown(t + 2)

        for n, (src, d, valid, passes, to) in enumerate(streams):
            c = t - d + 1

            @pl.when(jnp.logical_and(valid, jnp.logical_and(c >= 0, c < LAST)))
            def _():
                ref, sem = zref(src, c)
                wait_on(ref, sem)

                @pl.when(passes)
                def _():
                    zsend(ref, sem, n, c, to)

    def zsteps(lo, hi):
        @pl.loop(lo, hi)
        def _(t):
            zstep(t)

    def zdrain():
        ref, _ = zref(0, 0)
        for n in range(6):
            cond = is_src if n >= 4 else streams[n][3]

            @pl.when(cond)
            def _():
                for q in range(RING):
                    pltpu.make_async_copy(ref, ref, zs.at[n, q]).wait()

    def turn(a):
        @pl.loop(0, 4)
        def _(hh):
            rb = pl.multiple_of(((hh // 2) * 4 + a * 2 + hh % 2) * 128, 128)
            for xl in range(2):
                hi, lo = split(lbuf[a, xl, hh, 0:KL, :].T)
                lthi[pl.ds(rb, 128), xl * KL:(xl + 1) * KL] = hi
                ltlo[pl.ds(rb, 128), xl * KL:(xl + 1) * KL] = lo

    gcopy = remote(gsend, grecv, gsem.at[0], gsem.at[1], sib)

    def gram(rows, j):
        cols = slice(j * 512, j * 512 + 256)
        return nt(lthi[rows, :], lthi[cols, :]) + nt(lthi[rows, :], ltlo[cols, :]) + nt(ltlo[rows, :], lthi[cols, :])

    def lead_products():
        for j in range(2):
            for i in range(2):
                gsend[i * 256:i * 256 + 256, j * 256:j * 256 + 256] = gram(slice(i * 512, i * 512 + 256), j)
        gcopy.start()

    ii = lax.broadcasted_iota(jnp.int32, (128, 128), 0)
    jj = lax.broadcasted_iota(jnp.int32, (128, 128), 1)

    def lead_matrix():
        gcopy.wait()
        li[...] = gsend[...] + grecv[...]
        for h in range(4):
            c = slice(h * 128, (h + 1) * 128)
            li[c, c] += jnp.where(ii == jj, lbuf[0, 0, h, KL:KL + 1, :], 0.0)

    def sib_copy(a, g):
        rows = pl.ds(a * 256, 256)
        return remote(pbuf.at[g, rows], qbuf.at[g, rows], sx.at[a, g], xsem.at[a, g], sib)

    def product(a, g):
        for xl in range(2):
            for c in range(2):
                hi, lo = split(rbuf[c, (g // 4) * 2 + xl, g % 4])
                rh[xl * KL:(xl + 1) * KL, c * 128:(c + 1) * 128] = hi
                rl[xl * KL:(xl + 1) * KL, c * 128:(c + 1) * 128] = lo
        for t in range(2):
            q = (1 - p) if t == 0 else p
            rows = pl.ds(pl.multiple_of(q * 512 + a * 256, 256), 256)
            v = mm(lthi[rows, :], rh[...]) + mm(ltlo[rows, :], rh[...]) + mm(lthi[rows, :], rl[...])
            if t == 0:
                pbuf[g, a * 256:(a + 1) * 256, :] = v
                sib_copy(a, g).start()
            else:
                s_out[g, a * 256:(a + 1) * 256, :] = v

    def products(a, lo, hi):
        @pl.loop(lo, hi)
        def _(k):
            product(a, k)

    g_own = (x // 2) * 4 + y

    def combine(a, g):
        rows = slice(a * 256, a * 256 + 256)
        sib_copy(a, g).wait_recv()
        s_out[g, rows, :] = s_out[g, rows, :] + qbuf[g, rows, :]

    def add_diag(a):
        @pl.when(z // 2 == x_lo * 2 + p)
        def _():
            here = pl.ds(pl.multiple_of(a * 256 + (z % 2) * 128, 128), 128)
            diag = jnp.where(ii == jj, b[a, KL:KL + 1, :], 0.0)
            s_out[g_own, here, a * 128:(a + 1) * 128] += diag

    def piece(i, j):
        return li.at[pl.ds(pl.multiple_of(p * 256 + (i * 4 + j) * 16, 16), 16)]

    def l_copy(i, j, to_i, to_j, slot):
        ref = piece(i, j)
        return remote(ref, ref, lsend.at[slot], lrecv.at[i, j], plane(to_i, to_j))

    def l_scatter():
        for k in range(1, 16):
            go(l_copy(k // 4, k % 4, k // 4, k % 4, k), is_root)

    def l_arrived(i, j):
        wait_on(piece(i, j), lrecv.at[i, j], others)

    def l_along_x():
        l_arrived(x, y)
        for d in (1, 3, 2):
            go(l_copy(x, y, (x + d) % 4, y, 15 + d), not_root(x + d, y))

    def l_along_y():
        for e in range(4):
            i = (x + e) % 4
            if e:
                l_arrived(i, y)
            for d in (1, 3, 2):
                go(l_copy(i, y, x, (y + d) % 4, 18 + 3 * e + d), not_root(x, y + d))

    def l_finish():
        for d in (1, 3, 2):
            for e in range(4):
                l_arrived((x + e) % 4, (y + d) % 4)

    def on_root(f, *args):
        pl.when(is_root)(functools.partial(f, *args))

    def m_ref(i, a):
        return ms.at[i, pl.ds(a * 256, 256)]

    def m_first(a):
        @pl.when(z < 4)
        def _():
            ms[z % 4, a * 256:(a + 1) * 256, :] = s_out[0, a * 256:(a + 1) * 256, 0:128]

        for dr, to in ((0, zup), (1, zdn)):
            ref = m_ref(z % 4, a)
            go(remote(ref, ref, msend.at[a, 0, dr], mrecv.at[a, z % 4], to), z < 4)

    def m_forward(a, d):
        for dr, to in ((0, zup), (1, zdn)):
            i = (z + 8 - d) % 8 if dr == 0 else (z + d) % 8
            reach = up_of(i) if dr == 0 else 7 - up_of(i)
            ref, sem = m_ref(i % 4, a), mrecv.at[a, i % 4]
            wait_on(ref, sem, jnp.logical_and(i < 4, d <= reach))
            if d < 5:
                go(remote(ref, ref, msend.at[a, d, dr], sem, to), jnp.logical_and(i < 4, d < reach))

    def lead_zero():
        for i in range(3):
            li[i * 128:(i + 1) * 128, (i + 1) * 128:512] = jnp.zeros((128, 384 - 128 * i), F32)

    def combines(a, lo, hi):
        @pl.loop(lo, hi)
        def _(g):
            combine(a, g)

    def w_scatter():
        @pl.when(is_root)
        def _():
            for g in range(8):
                for hl in range(2):
                    wbuf[p, g, hl] = s_out[g, hl * 128:(hl + 1) * 128, :]

        for k in range(1, 16):
            ref = wbuf.at[p, k // 2, k % 2]
            go(remote(ref, ref, wsc.at[k], wrc.at[0], plane(k // 4, k % 4)), is_root)

    def both(f, *args):
        for a in range(2):
            f(a, *args)

    wcopy = remote(wbuf.at[p], wbuf.at[p], wsib.at[0], wsib.at[1], sib)
    mine_half = li.at[pl.ds(own_p, 256)]
    lcopy = remote(mine_half, mine_half, lsib.at[0], lsib.at[1], sib)

    zown(0)
    zown(1)
    both(right.second, 0, 0)
    zsteps(0, 3)
    both(right.second, 1, 1)
    both(right.second, 2, 3)
    zsteps(3, 4)
    both(right.second, 3, 2)
    both(right.forward, 0, 0)
    zsteps(4, 5)
    both(right.forward, 1, 1)
    zsteps(5, 7)
    both(right.forward, 2, 3)
    zsteps(7, 9)
    both(right.forward, 3, 2)
    zsteps(9, 10)
    turn(0)
    on_root(lead_products)
    zsteps(10, 11)
    for d in (0, 1, 3, 2):
        both(right.last, d)
    products(0, 0, 4)
    zsteps(11, 12)
    products(0, 4, 8)
    combines(0, 0, 8)
    add_diag(0)
    w_scatter()
    zsteps(12, 13)
    m_first(0)
    on_root(lead_matrix)
    on_root(factor_step, li, tile, 0)
    zsteps(13, 14)
    m_forward(0, 1)
    wait_on(wbuf.at[p, (x * 4 + y) // 2, y % 2], wrc.at[0], others)
    lead.first()
    both(lead.second, 0, 0)
    on_root(factor_step, li, tile, 1)
    zsteps(14, 15)
    m_forward(0, 2)
    both(lead.second, 1, 1)
    both(lead.second, 2, 3)
    on_root(factor_step, li, tile, 2)
    zsteps(15, 16)
    m_forward(0, 3)
    both(lead.second, 3, 2)
    both(lead.forward, 0, 0)
    turn(1)
    products(1, 0, 1)
    combines(1, 0, 1)
    pl.when(g_own == 0)(functools.partial(add_diag, 1))
    m_first(1)
    on_root(factor_step, li, tile, 3)
    on_root(lead_zero)
    l_scatter()
    m_forward(0, 4)
    both(lead.forward, 1, 1)
    products(1, 1, 3)
    m_forward(1, 1)
    both(lead.forward, 2, 3)
    both(lead.forward, 3, 2)
    products(1, 3, 5)
    m_forward(1, 2)
    m_forward(0, 5)
    l_along_x()
    products(1, 5, 7)
    m_forward(1, 3)
    for d in (0, 1, 3, 2):
        both(lead.last, d)
    wcopy.start()
    l_along_y()
    products(1, 7, 8)
    m_forward(1, 4)
    combines(1, 1, 8)
    pl.when(g_own != 0)(functools.partial(add_diag, 1))
    l_finish()
    pl.when(others)(lcopy.start)
    wait_on(wbuf.at[1 - p], wsib.at[1])
    wait_on(li.at[pl.ds(sib_p, 256)], lsib.at[1], others)

    hi, lo = split(li[...])
    lih[...] = hi
    lil[...] = lo

    @pl.loop(0, 8)
    def _(g):
        hs, ls = [], []
        for q in range(2):
            for hl in range(2):
                hi, lo = split(wbuf[q, g, hl])
                hs.append(hi)
                ls.append(lo)
        wh = jnp.concatenate(hs, axis=0)
        wl = jnp.concatenate(ls, axis=0)
        hi, lo = split(mm(lih[...], wh) + mm(lil[...], wh) + mm(lih[...], wl))
        fch[g] = hi
        fcl[g] = lo

    m_forward(1, 5)
    for k in range(4):
        krows = slice(k * 128, (k + 1) * 128)
        acc = jnp.zeros((512, 128), F32)
        for c in range(k + 1):
            hi, lo = split(ms[c])
            cc = slice(c * 128, (c + 1) * 128)
            acc += nt(hi, lih[krows, cc]) + nt(lo, lih[krows, cc]) + nt(hi, lil[krows, cc])
        ri = lax.broadcasted_iota(jnp.int32, (512, 128), 0)
        ki = lax.broadcasted_iota(jnp.int32, (512, 128), 1) + k * 128
        rows_at = (((ri // 256) * 8 + g_own) * 8 + (x_lo * 2 + p) * 2 + (ri // 128) % 2) * 128 + ri % 128
        acc = jnp.where(rows_at >= ki, acc, 0.0)
        hi, lo = split(acc)
        mfh[:, krows] = hi
        mfl[:, krows] = lo
        mf[k] = acc

    @pl.loop(0, 8)
    def _(g):
        for a in range(2):
            rows = slice(a * 256, (a + 1) * 256)
            v = mm(mfh[rows, :], fch[g]) + mm(mfl[rows, :], fch[g]) + mm(mfh[rows, :], fcl[g])
            sv = s_out[g, rows, :]
            v = jnp.where(jnp.logical_and(is_root, a == 0), sv, sv - v)
            for c in range(2):
                out[pl.ds(a * 256 * 16 + c * 8 + g, 256, stride=16), :] = v[:, c * 128:(c + 1) * 128]

    for c in range(4):
        @pl.when(z == c)
        def _():
            out[pl.ds(0, 512, stride=16), :] = mf[c]

    zdrain()
    for copy, cond in sends:
        if cond is None:
            copy.wait_send()
        else:
            pl.when(cond)(copy.wait_send)

    @pl.loop(0, 8)
    def _(g):
        for a in range(2):
            sib_copy(a, g).wait_send()

    wcopy.wait_send()
    pl.when(others)(lcopy.wait_send)


def schur_call(b):
    dma = pltpu.SemaphoreType.DMA
    vmem = pltpu.VMEM
    return pl.pallas_call(
        schur_kernel,
        out_shape=jax.ShapeDtypeStruct((8192, 128), F32),
        in_specs=[pl.BlockSpec(memory_space=pltpu.VMEM)],
        out_specs=pl.BlockSpec(memory_space=pltpu.VMEM),
        scratch_shapes=[
            vmem((2, 4, 4, KL, 128), F32), vmem((2, 2, 4, KP, 128), F32),
            vmem((1024, 2 * KL), BF16), vmem((1024, 2 * KL), BF16),
            vmem((2 * KL, 256), BF16), vmem((2 * KL, 256), BF16),
            vmem((8, 512, 256), F32), vmem((8, 512, 256), F32), vmem((8, 512, 256), F32),
            vmem((512, 512), F32), vmem((512, 512), F32), vmem((128, 128), F32),
            vmem((2, 8, 2, 128, 256), F32), vmem((512, 512), F32), vmem((4, 512, 128), F32), vmem((4, 512, 128), F32),
            vmem((512, 512), BF16), vmem((512, 512), BF16), vmem((512, 512), BF16), vmem((512, 512), BF16),
            vmem((8, 512, 256), BF16), vmem((8, 512, 256), BF16),
            dma((2, 3)), dma((2, 4, 2)), dma((2, 4, 2)), dma((2, 4, 4)), dma((2, 4, 2)),
            dma((2, 3)), dma((2, 4, 2)), dma((2, 4, 2)), dma((2, 4, 4)), dma((2, 4, 2)),
            dma((16,)), dma((1,)),
            dma((2,)), dma((2,)), dma((6, RING)), dma((2, 2, 4, NC)),
            dma((2, 8)), dma((2, 8)), dma((2,)), dma((31,)), dma((4, 4)), dma((2,)), dma((2,)),
            dma((2, 5, 2)), dma((2, 4)),
        ],
        compiler_params=pltpu.CompilerParams(
            collective_id=0, has_side_effects=True, vmem_limit_bytes=60 * 2**20
        ),
        name="schur_factor",
    )(b)


def scaled_blocks(link_block, block_mask, barrier_diag, first_section_diag):
    scen = block_mask.shape[0]
    w = block_mask.astype(F32).reshape(scen, 1, 2, 1) * jnp.sqrt(barrier_diag).reshape(scen, -1, 1, 1)
    v = (link_block.reshape(scen, -1, 2, 128) * w).reshape(KL, 2, 128).transpose(1, 0, 2)
    d = first_section_diag.reshape(2, 1, 128)
    return jnp.concatenate([v, d, jnp.zeros((2, KP - KL - 1, 128), F32)], axis=1)


def per_device(link_block, block_mask, barrier_diag, first_section_diag):
    b = scaled_blocks(link_block, block_mask, barrier_diag, first_section_diag)
    return schur_call(b).reshape(2, 1, 2, 128, 2, 8, 1, 128)


def solution(mesh):
    placed = (
        P("scen", None, "row", "col", None),
        P("scen", None, "row", "col"),
        P("scen"),
        P(None, "row", "col", None),
    )
    return jax.shard_map(
        per_device,
        mesh=mesh,
        in_specs=placed,
        out_specs=P(None, "row", "scen", None, None, None, "col", None),
        check_vma=False,
    )
```

time: 253 us -> 191 us (0.75)
  Pallas kernels: 240 us -> 179 us
    pallas_call x1, Pallas kernels: 240 us -> 179 us  [schur_call(): pl.pallas_call(schur_kernel, out_shape=jax.ShapeDtypeStruct((8192, 128),...]
where the time goes in v2:
time: 191 us
  Pallas kernels  179 us (94%)
  local copies, waits for them, and re-layouts  8.69 us (5%)
  other arithmetic  3.68 us (2%)
    pallas_call x1, Pallas kernels, schur_call(): pl.pallas_call(schur_kernel, out_shape=jax.ShapeDtypeStruct((8192, 128),...  179 us
    unnamed x1, local copies, waits for them, and re-layouts  7.77 us

profile of v2, /device:TPU:5, one launch (start us, length us, event | category | flops | bytes accessed | tf_op | source)
XLA Modules:
  0.0 191.0 jit_solution(888633307737991015)
XLA Ops:
  0.0 0.7 convert_element_type.3
  0.7 0.1 pad.2.clone
  0.8 0.7 sqrt.3
  1.5 0.1 mul.32
  1.5 0.1 mul.33
  1.6 1.3 fusion
  3.0 1.7 maximum_maximum_fusion.b
  4.6 178.6 %schur_factor.1 = f32[8192,128]{1,0:T(8,128)} custom-call(f32[2,648,128]{2,1,0:T(8,128)} %maximum_maximum_fusion.b), custom_call_target="tpu_custom_call" | custom-call | tf_op jit(solution)/shard_map/schur_factor/pallas_call | solution.py:587
  183.2 7.8 %copy.9 = f32[2,1,2,128,2,8,1,128]{7,6,5,4,3,2,1,0:T(1,128)} copy(f32[2,1,2,128,2,8,1,128]{7,6,5,4,3,2,1,0:T(1,128)} %bitcast.13) | data formatting | bytes 8388608
  (2 shorter events, 0.0 us)

commit v3 on v2

--- a/solution.py
+++ b/solution.py
@@ -323,15 +323,14 @@
                 hi, lo = split(rbuf[c, (g // 4) * 2 + xl, g % 4])
                 rh[xl * KL:(xl + 1) * KL, c * 128:(c + 1) * 128] = hi
                 rl[xl * KL:(xl + 1) * KL, c * 128:(c + 1) * 128] = lo
+        tiles = []
         for t in range(2):
             q = (1 - p) if t == 0 else p
             rows = pl.ds(pl.multiple_of(q * 512 + a * 256, 256), 256)
-            v = mm(lthi[rows, :], rh[...]) + mm(ltlo[rows, :], rh[...]) + mm(lthi[rows, :], rl[...])
-            if t == 0:
-                pbuf[g, a * 256:(a + 1) * 256, :] = v
-                sib_copy(a, g).start()
-            else:
-                s_out[g, a * 256:(a + 1) * 256, :] = v
+            tiles.append(mm(lthi[rows, :], rh[...]) + mm(ltlo[rows, :], rh[...]) + mm(lthi[rows, :], rl[...]))
+        s_out[g, a * 256:(a + 1) * 256, :] = tiles[1]
+        pbuf[g, a * 256:(a + 1) * 256, :] = tiles[0]
+        sib_copy(a, g).start()
 
     def products(a, lo, hi):
         @pl.loop(lo, hi)
@@ -469,51 +468,50 @@
     on_root(factor_step, li, tile, 0)
     zsteps(13, 14)
     m_forward(0, 1)
+    on_root(factor_step, li, tile, 1)
+    zsteps(14, 15)
+    m_forward(0, 2)
+    on_root(factor_step, li, tile, 2)
+    zsteps(15, 16)
+    m_forward(0, 3)
+    on_root(factor_step, li, tile, 3)
+    on_root(lead_zero)
+    l_scatter()
     wait_on(wbuf.at[p, (x * 4 + y) // 2, y % 2], wrc.at[0], others)
     lead.first()
     both(lead.second, 0, 0)
-    on_root(factor_step, li, tile, 1)
-    zsteps(14, 15)
-    m_forward(0, 2)
-    both(lead.second, 1, 1)
-    both(lead.second, 2, 3)
-    on_root(factor_step, li, tile, 2)
-    zsteps(15, 16)
-    m_forward(0, 3)
-    both(lead.second, 3, 2)
-    both(lead.forward, 0, 0)
     turn(1)
     products(1, 0, 1)
     combines(1, 0, 1)
     pl.when(g_own == 0)(functools.partial(add_diag, 1))
     m_first(1)
-    on_root(factor_step, li, tile, 3)
-    on_root(lead_zero)
-    l_scatter()
     m_forward(0, 4)
-    both(lead.forward, 1, 1)
+    both(lead.second, 1, 1)
+    both(lead.second, 2, 3)
+    both(lead.second, 3, 2)
+    l_along_x()
+    both(lead.forward, 0, 0)
     products(1, 1, 3)
     m_forward(1, 1)
+    both(lead.forward, 1, 1)
     both(lead.forward, 2, 3)
+    l_along_y()
     both(lead.forward, 3, 2)
+    m_forward(1, 2)
     products(1, 3, 5)
-    m_forward(1, 2)
     m_forward(0, 5)
-    l_along_x()
-    products(1, 5, 7)
     m_forward(1, 3)
+    l_finish()
+    pl.when(others)(lcopy.start)
     for d in (0, 1, 3, 2):
         both(lead.last, d)
     wcopy.start()
-    l_along_y()
-    products(1, 7, 8)
     m_forward(1, 4)
+    products(1, 5, 8)
     combines(1, 1, 8)
     pl.when(g_own != 0)(functools.partial(add_diag, 1))
-    l_finish()
-    pl.when(others)(lcopy.start)
+    wait_on(li.at[pl.ds(sib_p, 256)], lsib.at[1], others)
     wait_on(wbuf.at[1 - p], wsib.at[1])
-    wait_on(li.at[pl.ds(sib_p, 256)], lsib.at[1], others)
 
     hi, lo = split(li[...])
     lih[...] = hi

time: 191 us -> 174 us (0.911); the launches traced: 191 us -> 172 us
  Pallas kernels: 179 us -> 160 us
    pallas_call x1, Pallas kernels: 179 us -> 160 us  [schur_call(): pl.pallas_call(schur_kernel, out_shape=jax.ShapeDtypeStruct((8192, 128),...]
where the time goes in v3:
time: 174 us; the launch traced here: 172 us
  Pallas kernels  160 us (92%)
  local copies, waits for them, and re-layouts  8.69 us (5%)
  other arithmetic  3.68 us (2%)
    pallas_call x1, Pallas kernels, schur_call(): pl.pallas_call(schur_kernel, out_shape=jax.ShapeDtypeStruct((8192, 128),...  160 us
    unnamed x1, local copies, waits for them, and re-layouts  7.77 us

profile of v3, /device:TPU:5, one launch (start us, length us, event | category | flops | bytes accessed | tf_op | source)
XLA Modules:
  0.0 172.1 jit_solution(7416343147426248425)
XLA Ops:
  0.0 0.7 convert_element_type.3
  0.7 0.1 pad.2.clone
  0.8 0.7 sqrt.3
  1.5 0.1 mul.32
  1.5 0.1 mul.33
  1.6 1.3 fusion
  3.0 1.7 maximum_maximum_fusion.b
  4.6 159.6 %schur_factor.1 = f32[8192,128]{1,0:T(8,128)} custom-call(f32[2,648,128]{2,1,0:T(8,128)} %maximum_maximum_fusion.b), custom_call_target="tpu_custom_call" | custom-call | tf_op jit(solution)/shard_map/schur_factor/pallas_call | solution.py:585
  164.3 7.8 %copy.9 = f32[2,1,2,128,2,8,1,128]{7,6,5,4,3,2,1,0:T(1,128)} copy(f32[2,1,2,128,2,8,1,128]{7,6,5,4,3,2,1,0:T(1,128)} %bitcast.13) | data formatting | bytes 8388608
  (2 shorter events, 0.0 us)

commit v4 on v3

--- a/solution.py
+++ b/solution.py
@@ -610,6 +610,22 @@
     )(b)
 
 
+def hand_over(src, dst):
+    dst[...] = src[...]
+
+
+def hand_over_call(v):
+    spec = pl.BlockSpec((2048, 128), lambda i: (i, 0))
+    return pl.pallas_call(
+        hand_over,
+        grid=(4,),
+        out_shape=jax.ShapeDtypeStruct(v.shape, v.dtype),
+        in_specs=[spec],
+        out_specs=spec,
+        name="hand_over",
+    )(v)
+
+
 def scaled_blocks(link_block, block_mask, barrier_diag, first_section_diag):
     scen = block_mask.shape[0]
     w = block_mask.astype(F32).reshape(scen, 1, 2, 1) * jnp.sqrt(barrier_diag).reshape(scen, -1, 1, 1)
@@ -620,7 +636,7 @@
 
 def per_device(link_block, block_mask, barrier_diag, first_section_diag):
     b = scaled_blocks(link_block, block_mask, barrier_diag, first_section_diag)
-    return schur_call(b).reshape(2, 1, 2, 128, 2, 8, 1, 128)
+    return hand_over_call(schur_call(b)).reshape(2, 1, 2, 128, 2, 8, 1, 128)
 
 
 def solution(mesh):

time: 174 us -> 171 us (0.983)
  local copies, waits for them, and re-layouts: 8.69 us -> 0.92 us
  Pallas kernels: 160 us -> 164 us
    unnamed x1 -> x0, local copies, waits for them, and re-layouts: 7.77 us -> none
    pallas_call x0 -> x1, Pallas kernels: none -> 4.74 us  [hand_over_call(): pl.pallas_call(hand_over, grid=(4,), out_shape=jax.ShapeDtypeStruct(v.sha...]
where the time goes in v4:
time: 171 us; the launch traced here: 169 us
  Pallas kernels  164 us (96%)
  other arithmetic  3.68 us (2%)
    pallas_call x1, Pallas kernels, schur_call(): pl.pallas_call(schur_kernel, out_shape=jax.ShapeDtypeStruct((8192, 128),...  160 us
    pallas_call x1, Pallas kernels, hand_over_call(): pl.pallas_call(hand_over, grid=(4,), out_shape=jax.ShapeDtypeStruct(v.sha...  4.74 us

profile of v4, /device:TPU:5, one launch (start us, length us, event | category | flops | bytes accessed | tf_op | source)
XLA Modules:
  0.0 169.0 jit_solution(2818315285865780664)
XLA Ops:
  0.0 0.7 convert_element_type.3
  0.7 0.1 pad.2.clone
  0.8 0.7 sqrt.3
  1.5 0.1 mul.32
  1.5 0.1 mul.33
  1.6 1.3 fusion
  3.0 1.7 maximum_maximum_fusion.b
  4.6 159.6 %schur_factor.1.src = f32[8192,128]{1,0:T(8,128)} custom-call(f32[2,648,128]{2,1,0:T(8,128)} %maximum_maximum_fusion.b), custom_call_target="tpu_custom_call" | custom-call | tf_op jit(solution)/shard_map/schur_factor/pallas_call | solution.py:585
  164.3 4.7 %hand_over.1 = f32[8192,128]{1,0:T(8,128)} custom-call(f32[8192,128]{1,0:T(8,128)} %schur_factor.1.src), custom_call_target="tpu_custom_call" | custom-call | tf_op jit(solution)/shard_map/hand_over/pallas_call | solution.py:619
  (2 shorter events, 0.0 us)
